TPU v7x, 256 devices: a whole 4x4x8 slice. The times are simulated.
256 devices in a mesh: ctx: 16 (over y, x), head: 8 (over z), pipe: 2 (over core).
Axes of the slice: x: 4, y: 4, z: 8, core: 2. Of those that a mesh axis runs over, the one named last changes fastest.
Arguments:
- queries: bfloat16 [2, 2048, 8192], P('pipe', 'ctx', 'head'), may hold values from -6 to 6
- keys: bfloat16 [2, 2048, 8192], P('pipe', 'ctx', 'head'), may hold values from -6 to 6
- values: bfloat16 [2, 2048, 8192], P('pipe', 'ctx', 'head'), may hold values from -6 to 6
- gates: bfloat16 [2, 2048, 8192], P('pipe', 'ctx', 'head'), may hold values from -6 to 6
- log_decay: float32 [2, 2048, 64], P('pipe', 'ctx', 'head'), may hold values from -1 to 0
- segment_ids: int32 [2, 2048], P('pipe', 'ctx'), may hold values from 0 to 7, never falling along the last dimension, each value on 1 to 512 neighbouring positions
- norm_gain: float32 [2, 8192], P('pipe', 'head'), may hold values from 0.1 to 1.9
- out_weight: bfloat16 [2, 8192, 6144], P('pipe', 'head', 'ctx'), may hold values from -0.0625 to 0.0625
Outputs:
- handed: bfloat16 [2, 2048, 6144], P('pipe', 'ctx', 'head')
Inputs may be any that keep to these rules, and one draw needn't show every extreme that they name: `segment_ids`: along each section's tokens the ids never fall; a document has at most a quarter of 2048 tokens, and one has exactly that many.
All inputs are finite; a program needn't handle non-finite values.
Results may differ from a plain program's by a relative error of at most 0.02.
Values may be sent and summed in bfloat16 or wider, within the bound.
A program may use at most 64 MiB of HBM per device.

v0:
```python
import jax
import jax.numpy as jnp
from jax import lax
from jax.sharding import PartitionSpec as P

DH = 128
highest = lax.Precision.HIGHEST


def entering(shard, axis, combine, identity):
    count, index = (lax.axis_size(axis), lax.axis_index(axis))
    everything = jax.tree.map(
        lambda part, kind: lax.all_gather(part.astype(kind), axis),
        shard,
        (jnp.bfloat16, jnp.bfloat16, jnp.bfloat16),
    )
    start = jax.tree.map(
        lambda part, zero: jnp.broadcast_to(jnp.asarray(zero, part.dtype), part.shape),
        shard,
        identity,
    )

    def hop(k, before):
        reached = k < index
        new = combine(
            before, jax.tree.map(lambda part, own: part[k].astype(own.dtype), everything, shard)
        )
        return jax.tree.map(lambda a, b: jnp.where(reached, a, b), new, before)

    return lax.fori_loop(0, count, hop, start)


def from_behind(shard, axis, by):
    count = lax.axis_size(axis)
    return lax.ppermute(shard, axis, [(i, (i + by) % count) for i in range(count)])


def block_step(carried, pieces):
    kv_state, doc_id = carried
    query_rows, key_rows, value_rows, rate_rows, doc_rows = pieces
    length = doc_rows.shape[0]
    running = jnp.cumsum(rate_rows, axis=0)
    running_t = running.T
    causal = lax.broadcasted_iota(jnp.int32, (length, length), 0) >= lax.broadcasted_iota(
        jnp.int32, (length, length), 1
    )
    allowed = causal & (doc_rows[:, None] == doc_rows[None, :])
    log_gaps = running_t[:, :, None] - running_t[:, None, :]
    weights = jnp.where(allowed[None], jnp.exp(jnp.where(allowed[None], log_gaps, 0.0)), 0.0)
    scores = jnp.einsum("ihd,jhd->hij", query_rows, key_rows, preferred_element_type=jnp.float32)
    mixed = (scores * weights).astype(jnp.bfloat16)
    inside = jnp.einsum("hij,jhd->ihd", mixed, value_rows, preferred_element_type=jnp.float32)
    value_full = value_rows.astype(jnp.float32)
    reaches = jnp.exp(running) * (doc_rows == doc_id).astype(jnp.float32)[:, None]
    carried_part = jnp.einsum(
        "ihd,hde->ihe",
        query_rows.astype(jnp.float32) * reaches[:, :, None],
        kv_state,
        precision=highest,
    )
    final_doc = doc_rows[-1]
    retain = (doc_id == final_doc).astype(jnp.float32)
    fading = (
        jnp.exp(running[-1][None, :] - running)
        * (doc_rows == final_doc).astype(jnp.float32)[:, None]
    )
    fresh_part = jnp.einsum(
        "jhd,jhe->hde",
        key_rows.astype(jnp.float32) * fading[:, :, None],
        value_full,
        precision=highest,
    )
    new_state = retain * jnp.exp(running[-1])[:, None, None] * kv_state + fresh_part
    return ((new_state, final_doc), inside + carried_part)


def sweep(query3, key3, value3, rate_rows, doc_rows, start_state, start_doc):
    rows_here = doc_rows.shape[0]
    heads_here = query3.shape[1]
    block_len = min(512, rows_here)
    block_count = rows_here // block_len
    pieces = (
        query3.reshape(block_count, block_len, heads_here, DH),
        key3.reshape(block_count, block_len, heads_here, DH),
        value3.reshape(block_count, block_len, heads_here, DH),
        rate_rows.reshape(block_count, block_len, heads_here),
        doc_rows.reshape(block_count, block_len),
    )
    final_carry, attended = lax.scan(block_step, (start_state, start_doc), pieces)
    return (final_carry[0], attended.reshape(rows_here, heads_here, DH))


def combine_pair(earlier, later):
    rate_early, state_early, doc_early = earlier
    rate_late, state_late, doc_late = later
    linked = ((doc_early == doc_late) | (doc_early < 0) | (doc_late < 0)).astype(jnp.float32)
    merged = linked[0] * rate_late[:, None, None] * state_early + state_late
    return (rate_early * rate_late, merged, jnp.where(doc_late < 0, doc_early, doc_late))


def carry_in(shard_rates, shard_state, shard_doc):
    heads_here = shard_rates.shape[0]
    neutral = (
        jnp.ones((heads_here,), jnp.float32),
        jnp.zeros((heads_here, DH, DH), jnp.float32),
        jnp.full((1,), -1.0, jnp.float32),
    )
    prefix = entering((shard_rates, shard_state, shard_doc), "ctx", combine_pair, neutral)
    return (prefix[1], prefix[2])


def on_device(queries, keys, values, gates, log_decay, segment_ids, norm_gain, out_weight):
    rows_here = queries.shape[1]
    width = queries.shape[2]
    heads_here = width // DH
    query3 = queries[0].reshape(rows_here, heads_here, DH)
    key3 = keys[0].reshape(rows_here, heads_here, DH)
    value3 = values[0].reshape(rows_here, heads_here, DH)
    rate_rows = log_decay[0]
    doc_rows = segment_ids[0].astype(jnp.float32)
    running = jnp.cumsum(rate_rows, axis=0)
    shard_rates = jnp.exp(running[-1])
    shard_doc = doc_rows[-1:]
    fading = (
        jnp.exp(running[-1][None, :] - running)
        * (doc_rows == shard_doc[0]).astype(jnp.float32)[:, None]
    )
    shard_state = jnp.einsum(
        "jhd,jhe->hde",
        key3.astype(jnp.float32) * fading[:, :, None],
        value3.astype(jnp.float32),
        precision=highest,
    )
    incoming, incoming_doc = carry_in(shard_rates, shard_state, shard_doc)
    ignored, attended = sweep(query3, key3, value3, rate_rows, doc_rows, incoming, incoming_doc[0])
    scaling = lax.rsqrt(jnp.mean(attended * attended, axis=-1, keepdims=True) + 1e-06)
    normed = (
        (attended * scaling).reshape(rows_here, width)
        * norm_gain[0][None, :]
        * jax.nn.sigmoid(gates[0].astype(jnp.float32))
    ).astype(jnp.bfloat16)
    weight_here = out_weight[0]
    partial_value = jnp.dot(
        normed,
        lax.all_gather(weight_here, "ctx", axis=1, tiled=True),
        preferred_element_type=jnp.float32,
    )
    summed = lax.psum_scatter(
        partial_value.astype(jnp.bfloat16), "head", scatter_dimension=1, tiled=True
    )
    handed = from_behind(summed, "pipe", 1)
    return handed[None]


def solution(mesh):
    return jax.shard_map(
        on_device,
        mesh=mesh,
        in_specs=(
            P("pipe", "ctx", "head"),
            P("pipe", "ctx", "head"),
            P("pipe", "ctx", "head"),
            P("pipe", "ctx", "head"),
            P("pipe", "ctx", "head"),
            P("pipe", "ctx"),
            P("pipe", "head"),
            P("pipe", "head", "ctx"),
        ),
        out_specs=P("pipe", "ctx", "head"),
        check_vma=False,
    )
```

profile of v0, /device:TPU:1, one launch (start us, length us, event | category | flops | bytes accessed | tf_op | source)
XLA Modules:
  0.0 237.9 jit_solution(17835527506379368174)
XLA Ops:
  6.5 0.8 copy.22
  7.3 0.2 reduce_window_sum.13
  7.5 0.7 convert_bitcast_fusion.1
  8.2 0.6 slice.13
  8.8 1.3 compare_convert_fusion.1
  10.1 0.1 exponential_multiply_fusion.1
  10.2 1.1 copy.36
  11.3 1.0 copy.39
  12.3 1.1 convolution_convert_fusion
  13.5 0.0 all-gather.6.cloned.1.call-update
  13.5 0.0 all-gather.8.cloned.1.call-start
  13.5 0.7 all-gather.8.cloned.1.call-update
  14.2 0.0 reduce-scatter.2.cloned.1.call-start
  15.0 1.3 dynamic-slice.1
  16.2 0.8 dynamic-update-slice
  17.0 34.4 %all-reduce = bf16[16]{0:T(256)(128)(2,1)S(1)} all-reduce(bf16[16]{0:T(256)(128)(2,1)S(1)} %dynamic-update-slice), channel_id=1, replica_groups=mesh['ctx'=16,'head'=8,'pipe'=2] {'ctx'}, use_global_device_ids=true, to_apply=%add | all-reduce | flops 16 | bytes 64
  51.4 14.6 %all-gather.2 = bf16[16,1,8]{2,1,0:T(2,128)(2,1)S(1)} all-gather(bf16[1,1,8]{2,1,0:T(2,128)(2,1)S(1)} %get-tuple-element.212), channel_id=1, replica_groups=mesh['ctx'=16,'head'=8,'pipe'=2] {'ctx'}, dimensions={0}, use_global_device_ids=true | all-gather | bytes 272 | tf_op jit(solution)/shard_map/all_gather | solution.py:13
  65.9 1.0 copy.38
  67.0 0.1 fusion.34
  67.1 7.1 %all-gather.6.cloned.1.call-done = bf16[128,128,128]{2,1,0:T(8,128)(2,1)} async-done(((bf16[8,128,128]{2,1,0:T(8,128)(2,1)}), bf16[128,128,128]{2,1,0:T(8,128)(2,1)}) %all-gather.6.cloned.1.call-update) | async-done | bytes 4194320 | tf_op jit(solution)/shard_map/all_gather | solution.py:13
  74.2 62.4 %while.10 = (s32[]{:T(128)}, f32[8,128,128]{2,1,0:T(8,128)S(1)}, f32[1]{0:T(128)}, s32[]{:T(128)}, bf16[16,1]{0,1:T(2,128)(2,1)S(1)}, /*index=5*/bf16[16,8]{1,0:...) while((s32[]{:T(128)}, f32[8,128,128]{2,1,0:T(8,128)S(1)}, ...), condition=%wide.region_2.3_spmd.clone, body=%wide.region_1.2_spmd.clone.sunk | while | flops 655388 | bytes 1310999 | solution.py:30
  74.2 0.7 constant_dynamic-slice_fusion.3
  76.3 1.1 fusion.44
  78.1 0.7 constant_dynamic-slice_fusion.3
  80.2 1.1 fusion.44
  82.0 0.7 constant_dynamic-slice_fusion.3
  84.1 1.1 fusion.44
  85.9 0.7 constant_dynamic-slice_fusion.3
  88.0 1.1 fusion.44
  89.8 0.7 constant_dynamic-slice_fusion.3
  91.9 1.1 fusion.44
  93.7 0.7 constant_dynamic-slice_fusion.3
  95.8 1.1 fusion.44
  97.6 0.7 constant_dynamic-slice_fusion.3
  99.7 1.1 fusion.44
  101.5 0.7 constant_dynamic-slice_fusion.3
  103.6 1.1 fusion.44
  105.4 0.7 constant_dynamic-slice_fusion.3
  107.5 1.1 fusion.44
  109.3 0.7 constant_dynamic-slice_fusion.3
  111.4 1.1 fusion.44
  113.2 0.7 constant_dynamic-slice_fusion.3
  115.3 1.1 fusion.44
  117.1 0.7 constant_dynamic-slice_fusion.3
  119.2 1.1 fusion.44
  121.0 0.7 constant_dynamic-slice_fusion.3
  123.1 1.1 fusion.44
  124.9 0.7 constant_dynamic-slice_fusion.3
  127.0 1.1 fusion.44
  128.8 0.7 constant_dynamic-slice_fusion.3
  130.9 1.1 fusion.44
  132.7 0.7 constant_dynamic-slice_fusion.3
  134.8 1.1 fusion.44
  136.7 0.1 exponential_multiply_fusion
  136.8 1.3 convolution_bitcast_fusion.1
  138.1 0.5 multiply_reduce_fusion
  138.7 0.2 copy.34
  138.9 41.3 %all-gather.8.cloned.1.call-done = bf16[1,1024,6144]{2,1,0:T(8,128)(2,1)} async-done(((bf16[1,1024,384]{2,1,0:T(8,128)(2,1)}), bf16[1,1024,6144]{2,1,0:T(8,128)(2,1)}) %all-gather.8.cloned.1.call-update) | async-done | bytes 12582928 | tf_op jit(solution)/shard_map/all_gather | solution.py:145
  180.1 7.6 %fusion.6 = bf16[128,6144]{1,0:T(8,128)(2,1)} fusion(bf16[1,1024,6144]{2,1,0:T(8,128)(2,1)} %all-gather.8.cloned.1.call-done, bf16[1,128,1024]{2,1,0:T(8,128)(2,1)S(1)} %copy-done, f32[128,1024]{1,0:T(8,128)S(1)} %copy.34, f32[1024]{0:T(1024)S(1)} %bitcast.81), kind=kOutput, calls=%fused_computation.9 | convolution fusion | flops 1612316672 | bytes 14946304 | tf_op jit(solution)/shard_map/dot_general | solution.py:143
  187.8 0.0 reduce-scatter.2.cloned.1.call-update
  187.8 37.0 %reduce-scatter.2.cloned.1.call-done = bf16[128,768]{1,0:T(8,128)(2,1)} async-done(((bf16[128,6144]{1,0:T(8,128)(2,1)}), bf16[128,768]{1,0:T(8,128)(2,1)}) %reduce-scatter.2.cloned.1.call-update) | async-done | bytes 196624 | tf_op jit(solution)/shard_map/reduce_scatter | solution.py:148
  224.8 4.6 %collective-permute-start = (bf16[128,768]{1,0:T(8,128)(2,1)}, bf16[128,768]{1,0:T(8,128)(2,1)S(1)}, u32[]{:S(2)}, u32[]{:S(2)}) collective-permute-start(bf16[128,768]{1,0:T(8,128)(2,1)} %reduce-scatter.2.cloned.1.call-done), channel_id=1, source_target_pairs={{0,1},{1,0},{2,3},{3,2},{4,5},{5,4},{6,7},{7,6},{8,9},{9,8},{10,11... | collective-permute-start | bytes 589832 | tf_op jit(solution)/shard_map/ppermute | solution.py:35
  229.4 1.3 collective-permute-done
  230.7 0.7 copy.70
  (33 shorter events, 0.5 us)
Async XLA Ops:
  6.5 67.7 %all-gather.6.cloned.1.call-start = ((), (), s32[]{:S(2)}) async-start(), calls=%async_computation.2 | async-start | bytes 4456448 | tf_op jit(solution)/shard_map/all_gather | solution.py:13
  13.5 123.2 %copy-start.2 = (s32[1,128]{1,0:T(1,128)S(1)}, s32[1,128]{1,0:T(1,128)}, u32[]{:S(2)}) copy-start(s32[1,128]{1,0:T(1,128)} %param.15) | copy-start | bytes 1540
  13.5 166.6 %all-gather.8.cloned.1.call-start = ((), (), s32[]{:S(2)}) async-start(), calls=%async_computation.3 | async-start | bytes 13369344 | tf_op jit(solution)/shard_map/all_gather | solution.py:145
  14.2 210.5 %reduce-scatter.2.cloned.1.call-start = ((), (), s32[]{:S(2)}) async-start(), calls=%async_computation.1 | async-start | bytes 1769472 | tf_op jit(solution)/shard_map/reduce_scatter | solution.py:148
  136.6 43.5 %copy-start = (bf16[1,128,1024]{2,1,0:T(8,128)(2,1)S(1)}, bf16[1,128,1024]{2,1,0:T(8,128)(2,1)}, u32[]{:S(2)}) copy-start(bf16[1,128,1024]{2,1,0:T(8,128)(2,1)} %param.13) | copy-start | bytes 786436
  136.6 43.5 %copy-start.1 = (f32[1,1024]{1,0:T(1,128)S(1)}, f32[1,1024]{1,0:T(1,128)}, u32[]{:S(2)}) copy-start(f32[1,1024]{1,0:T(1,128)} %param.16) | copy-start | bytes 12292
  224.8 5.9 %collective-permute-start = (bf16[128,768]{1,0:T(8,128)(2,1)}, bf16[128,768]{1,0:T(8,128)(2,1)S(1)}, u32[]{:S(2)}, u32[]{:S(2)}) collective-permute-start(bf16[128,768]{1,0:T(8,128)(2,1)} %reduce-scatter.2.cloned.1.call-done), channel_id=1, source_target_pairs={{0,1},{1,0},{2,3},{3,2},{4,5},{5,4},{6,7},{7,6},{8,9},{9,8},{10,11... | collective-permute-start | bytes 589832 | tf_op jit(solution)/shard_map/ppermute | solution.py:35
Sparse Core Ops, SparseCore 0:
  13.6 60.5 all-gather.5
  76.6 103.4 all-gather.7
  187.9 36.8 reduce-scatter.1
where the time goes:
time: 239 us; the launch traced here: 238 us
  waiting for transfers between devices  87.4 us (37%)
  blocking collectives  48.9 us (20%)
  loops' own time  34.1 us (14%)
  other arithmetic  20.2 us (8%)
  local copies, waits for them, and re-layouts  18.2 us (8%)
  between operations  13.9 us (6%)
  matrix products  10.5 us (4%)
  starting transfers between devices  4.7 us (2%)
    all_gather x1, waiting for transfers between devices, on_device(): lax.all_gather(weight_here, 'ctx', axis=1, tiled=True)  41.3 us
    reduce_scatter x1, waiting for transfers between devices, on_device(): lax.psum_scatter(partial_value.astype(jnp.bfloat16), 'head', scatter_dime...  37 us
    unnamed x1, blocking collectives  34.4 us
    another operation x1, loops' own time, entering(): return lax.fori_loop(0, count, hop, start)  34.1 us
    select_n x16, other arithmetic, hop(): return jax.tree.map(lambda a, b: jnp.where(reached, a, b), new, before)  17.5 us
    all_gather x1, blocking collectives, entering(): lax.all_gather(part.astype(kind), axis)  14.6 us
    dynamic_slice x16, local copies, waits for them, and re-layouts, hop(): part[k].astype(own.dtype)  10.6 us
    dot_general x1, matrix products, on_device(): jnp.dot(normed, lax.all_gather(weight_here, 'ctx', axis=1, tiled=True), p...  7.63 us
  transfers between devices with their start and end apart: 4, of which 4 were waited for; matrix products, arithmetic and copies ran while one was open for 14% of the time, Pallas kernels for 0%

commit v1 on v0

--- a/solution.py
+++ b/solution.py
@@ -5,6 +5,28 @@
 
 DH = 128
 highest = lax.Precision.HIGHEST
+
+
+def joined_along(blocks, dim):
+    blocks = jnp.moveaxis(blocks, 0, dim)
+    shape = blocks.shape
+    return blocks.reshape(*shape[:dim], shape[dim] * shape[dim + 1], *shape[dim + 2 :])
+
+
+def ring_gather(shard, axis, dim):
+    peers = lax.axis_size(axis)
+    pairs = [(i, (i + 1) % peers) for i in range(peers)]
+    back = [(b, a) for a, b in pairs]
+    lower, upper = ([], [])
+    for step in range(peers - 1):
+        if step % 2 == 0:
+            lower.append(lax.ppermute(lower[-1] if lower else shard, axis, pairs))
+        else:
+            upper.append(lax.ppermute(upper[-1] if upper else shard, axis, back))
+    blocks = jnp.stack([*lower[::-1], shard, *upper])
+    shift = lax.axis_index(axis) - len(lower)
+    blocks = blocks[(jnp.arange(peers) - shift) % peers]
+    return joined_along(blocks, dim)
 
 
 def entering(shard, axis, combine, identity):
@@ -141,9 +163,7 @@
     ).astype(jnp.bfloat16)
     weight_here = out_weight[0]
     partial_value = jnp.dot(
-        normed,
-        lax.all_gather(weight_here, "ctx", axis=1, tiled=True),
-        preferred_element_type=jnp.float32,
+        normed, ring_gather(weight_here, "ctx", 1), preferred_element_type=jnp.float32
     )
     summed = lax.psum_scatter(
         partial_value.astype(jnp.bfloat16), "head", scatter_dimension=1, tiled=True

time: 239 us -> 420 us (1.76)
  waiting for transfers between devices: 87.4 us -> 164 us
  local copies, waits for them, and re-layouts: 18.2 us -> 77.1 us
  starting transfers between devices: 4.7 us -> 40.2 us
  blocking collectives: 48.9 us -> 54.4 us
    ppermute x0 -> x15, waiting for transfers between devices: none -> 86.7 us  [the longest x8 64.3 us: ring_gather(): lower.append(lax.ppermute(lower[-1] if lower else shard, axis, pairs))]
    all_gather x1 -> x0, waiting for transfers between devices: 41.3 us -> none  [on_device(): lax.all_gather(weight_here, 'ctx', axis=1, tiled=True)]
    reduce_scatter x1, waiting for transfers between devices: 37 us -> 75.8 us  [on_device(): lax.psum_scatter(partial_value.astype(jnp.bfloat16), 'head', scatter_dime...]
    ppermute x0 -> x15, starting transfers between devices: none -> 35.4 us  [the longest x7 33.4 us: ring_gather(): upper.append(lax.ppermute(upper[-1] if upper else shard, axis, back))]
    unnamed x13 -> x48, local copies, waits for them, and re-layouts: 4.72 us -> 34.5 us
    transpose x0 -> x1, local copies, waits for them, and re-layouts: none -> 16.6 us  [joined_along(): blocks = jnp.moveaxis(blocks, 0, dim)]
    gather x0 -> x1, local copies, waits for them, and re-layouts: none -> 11.5 us  [ring_gather(): blocks = blocks[(jnp.arange(peers) - shift) % peers]]
    all_gather x1, waiting for transfers between devices: 7.12 us -> 0.01 us  [entering(): lax.all_gather(part.astype(kind), axis)]
  transfers between devices with their start and end apart: 4 -> 18, of which waited for: 4 -> 13; matrix products, arithmetic and copies ran while one was open for 14% -> 16% of each run, Pallas kernels for 0% -> 0%
where the time goes in v1:
time: 420 us; the launch traced here: 418 us
  waiting for transfers between devices  164 us (39%)
  local copies, waits for them, and re-layouts  77.1 us (18%)
  blocking collectives  54.4 us (13%)
  starting transfers between devices  40.2 us (10%)
  loops' own time  34 us (8%)
  other arithmetic  21.4 us (5%)
  between operations  14.3 us (3%)
  matrix products  12.9 us (3%)
    reduce_scatter x1, waiting for transfers between devices, on_device(): lax.psum_scatter(partial_value.astype(jnp.bfloat16), 'head', scatter_dime...  75.8 us
    ppermute x8, waiting for transfers between devices, ring_gather(): lower.append(lax.ppermute(lower[-1] if lower else shard, axis, pairs))  64.3 us
    unnamed x1, blocking collectives  37.4 us
    unnamed x48, local copies, waits for them, and re-layouts  34.5 us
    another operation x1, loops' own time, entering(): return lax.fori_loop(0, count, hop, start)  34 us
    ppermute x7, starting transfers between devices, ring_gather(): upper.append(lax.ppermute(upper[-1] if upper else shard, axis, back))  33.4 us
    ppermute x7, waiting for transfers between devices, ring_gather(): upper.append(lax.ppermute(upper[-1] if upper else shard, axis, back))  22.4 us
    select_n x16, other arithmetic, hop(): return jax.tree.map(lambda a, b: jnp.where(reached, a, b), new, before)  17.5 us
  transfers between devices with their start and end apart: 18, of which 13 were waited for; matrix products, arithmetic and copies ran while one was open for 16% of the time, Pallas kernels for 0%

profile of v1, /device:TPU:1, one launch (start us, length us, event | category | flops | bytes accessed | tf_op | source)
XLA Modules:
  0.0 418.0 jit_solution(5696145613551624040)
XLA Ops:
  6.5 2.0 collective-permute-start
  8.6 19.4 %collective-permute-done = bf16[1024,384]{1,0:T(8,128)(2,1)S(1)} collective-permute-done((bf16[1024,384]{1,0:T(8,128)(2,1)}, bf16[1024,384]{1,0:T(8,128)(2,1)S(1)}, u32[]{:S(2)}, u32[]{:S(2)}) %collective-permute-start) | collective-permute-done | bytes 786464 | tf_op jit(solution)/shard_map/ppermute | solution.py:23
  28.9 4.8 %collective-permute-start.8 = (bf16[1024,384]{1,0:T(8,128)(2,1)}, bf16[1024,384]{1,0:T(8,128)(2,1)S(1)}, u32[]{:S(2)}, u32[]{:S(2)}) collective-permute-start(bf16[1024,384]{1,0:T(8,128)(2,1)} %bitcast.107), channel_id=1, source_target_pairs={{16,0},{32,16},{48,32},{64,48},{80,64},{96,80},{112,96},{128,112},... | collective-permute-start | bytes 2359304 | tf_op jit(solution)/shard_map/ppermute | solution.py:25
  33.6 14.4 %collective-permute-done.1 = bf16[1024,384]{1,0:T(8,128)(2,1)S(1)} collective-permute-done((bf16[1024,384]{1,0:T(8,128)(2,1)S(1)}, bf16[1024,384]{1,0:T(8,128)(2,1)S(1)}, u32[]{:S(2)}, u32[]{:S(2)}) %collective-permute-start.1) | collective-permute-done | bytes 786464 | tf_op jit(solution)/shard_map/ppermute | solution.py:23
  50.3 1.3 compare_convert_fusion.1
  51.7 1.1 copy.69
  52.9 1.0 copy.71
  53.9 4.9 %collective-permute-start.9 = (bf16[1024,384]{1,0:T(8,128)(2,1)S(1)}, bf16[1024,384]{1,0:T(8,128)(2,1)}, u32[]{:S(2)}, u32[]{:S(2)}) collective-permute-start(bf16[1024,384]{1,0:T(8,128)(2,1)S(1)} %collective-permute-done.8), channel_id=1, source_target_pairs={{16,0},{32,16},{48,32},{64,48},{80,64},{96,80},{112,96},{128,112},... | collective-permute-start | bytes 2359304 | tf_op jit(solution)/shard_map/ppermute | solution.py:25
  58.8 7.7 %collective-permute-done.2 = bf16[1024,384]{1,0:T(8,128)(2,1)} collective-permute-done((bf16[1024,384]{1,0:T(8,128)(2,1)S(1)}, bf16[1024,384]{1,0:T(8,128)(2,1)}, u32[]{:S(2)}, u32[]{:S(2)}) %collective-permute-start.2) | collective-permute-done | bytes 786464 | tf_op jit(solution)/shard_map/ppermute | solution.py:23
  66.5 1.1 convolution_convert_fusion.1
  67.7 3.6 collective-permute-done.9
  71.3 5.6 %collective-permute-start.10 = (bf16[1024,384]{1,0:T(8,128)(2,1)}, bf16[1024,384]{1,0:T(8,128)(2,1)S(1)}, u32[]{:S(2)}, u32[]{:S(2)}) collective-permute-start(bf16[1024,384]{1,0:T(8,128)(2,1)} %collective-permute-done.9), channel_id=1, source_target_pairs={{16,0},{32,16},{48,32},{64,48},{80,64},{96,80},{112,96},{128,112},... | collective-permute-start | bytes 2359304 | tf_op jit(solution)/shard_map/ppermute | solution.py:25
  76.9 7.3 %collective-permute-done.3 = bf16[1024,384]{1,0:T(8,128)(2,1)} collective-permute-done((bf16[1024,384]{1,0:T(8,128)(2,1)}, bf16[1024,384]{1,0:T(8,128)(2,1)}, u32[]{:S(2)}, u32[]{:S(2)}) %collective-permute-start.3) | collective-permute-done | bytes 786464 | tf_op jit(solution)/shard_map/ppermute | solution.py:23
  84.2 4.6 %collective-permute-done.10 = bf16[1024,384]{1,0:T(8,128)(2,1)S(1)} collective-permute-done((bf16[1024,384]{1,0:T(8,128)(2,1)}, bf16[1024,384]{1,0:T(8,128)(2,1)S(1)}, u32[]{:S(2)}, u32[]{:S(2)}) %collective-permute-start.10) | collective-permute-done | bytes 786464 | tf_op jit(solution)/shard_map/ppermute | solution.py:25
  89.7 5.4 %collective-permute-start.11 = (bf16[1024,384]{1,0:T(8,128)(2,1)S(1)}, bf16[1024,384]{1,0:T(8,128)(2,1)S(1)}, u32[]{:S(2)}, u32[]{:S(2)}) collective-permute-start(bf16[1024,384]{1,0:T(8,128)(2,1)S(1)} %collective-permute-done.10), channel_id=1, source_target_pairs={{16,0},{32,16},{48,32},{64,48},{80,64},{96,80},{112,96},{128,112},... | collective-permute-start | bytes 2359304 | tf_op jit(solution)/shard_map/ppermute | solution.py:25
  95.1 8.6 %collective-permute-done.4 = bf16[1024,384]{1,0:T(8,128)(2,1)S(1)} collective-permute-done((bf16[1024,384]{1,0:T(8,128)(2,1)}, bf16[1024,384]{1,0:T(8,128)(2,1)S(1)}, u32[]{:S(2)}, u32[]{:S(2)}) %collective-permute-start.4) | collective-permute-done | bytes 786464 | tf_op jit(solution)/shard_map/ppermute | solution.py:23
  103.7 6.4 %collective-permute-done.11 = bf16[1024,384]{1,0:T(8,128)(2,1)S(1)} collective-permute-done((bf16[1024,384]{1,0:T(8,128)(2,1)S(1)}, bf16[1024,384]{1,0:T(8,128)(2,1)S(1)}, u32[]{:S(2)}, u32[]{:S(2)}) %collective-permute-start.11) | collective-permute-done | bytes 786464 | tf_op jit(solution)/shard_map/ppermute | solution.py:25
  111.0 5.5 %collective-permute-start.12 = (bf16[1024,384]{1,0:T(8,128)(2,1)S(1)}, bf16[1024,384]{1,0:T(8,128)(2,1)}, u32[]{:S(2)}, u32[]{:S(2)}) collective-permute-start(bf16[1024,384]{1,0:T(8,128)(2,1)S(1)} %collective-permute-done.11), channel_id=1, source_target_pairs={{16,0},{32,16},{48,32},{64,48},{80,64},{96,80},{112,96},{128,112},... | collective-permute-start | bytes 2359304 | tf_op jit(solution)/shard_map/ppermute | solution.py:25
  116.6 3.2 collective-permute-done.5
  119.7 7.8 %collective-permute-done.12 = bf16[1024,384]{1,0:T(8,128)(2,1)} collective-permute-done((bf16[1024,384]{1,0:T(8,128)(2,1)S(1)}, bf16[1024,384]{1,0:T(8,128)(2,1)}, u32[]{:S(2)}, u32[]{:S(2)}) %collective-permute-start.12) | collective-permute-done | bytes 786464 | tf_op jit(solution)/shard_map/ppermute | solution.py:25
  127.5 5.6 %collective-permute-start.13 = (bf16[1024,384]{1,0:T(8,128)(2,1)}, bf16[1024,384]{1,0:T(8,128)(2,1)}, u32[]{:S(2)}, u32[]{:S(2)}) collective-permute-start(bf16[1024,384]{1,0:T(8,128)(2,1)} %collective-permute-done.12), channel_id=1, source_target_pairs={{16,0},{32,16},{48,32},{64,48},{80,64},{96,80},{112,96},{128,112},... | collective-permute-start | bytes 2359304 | tf_op jit(solution)/shard_map/ppermute | solution.py:25
  133.1 3.7 collective-permute-done.6
  137.5 1.3 dynamic-slice.1
  139.5 37.4 %all-reduce = bf16[16]{0:T(256)(128)(2,1)S(1)} all-reduce(bf16[16]{0:T(256)(128)(2,1)S(1)} %dynamic-update-slice), channel_id=1, replica_groups=mesh['ctx'=16,'head'=8,'pipe'=2] {'ctx'}, use_global_device_ids=true, to_apply=%add | all-reduce | flops 16 | bytes 64
  176.9 17.0 %all-gather.1 = bf16[16,1,8]{2,1,0:T(2,128)(2,1)S(1)} all-gather(bf16[1,1,8]{2,1,0:T(2,128)(2,1)S(1)} %get-tuple-element.226), channel_id=1, replica_groups=mesh['ctx'=16,'head'=8,'pipe'=2] {'ctx'}, dimensions={0}, use_global_device_ids=true | all-gather | bytes 272 | tf_op jit(solution)/shard_map/all_gather | solution.py:35
  193.9 1.0 copy.70
  195.0 1.1 add_divide_fusion
  196.5 1.5 collective-permute-start.14
  198.0 2.1 bitcast_dynamic-update-slice_fusion.14
  200.1 2.1 bitcast_dynamic-update-slice_fusion.13
  202.2 2.1 bitcast_dynamic-update-slice_fusion.12
  204.3 2.1 bitcast_dynamic-update-slice_fusion.11
  206.5 2.1 bitcast_dynamic-update-slice_fusion.10
  208.6 2.1 bitcast_dynamic-update-slice_fusion.9
  210.7 2.1 bitcast_dynamic-update-slice_fusion.8
  212.8 2.1 bitcast_dynamic-update-slice_fusion.7
  216.8 2.2 bitcast_dynamic-update-slice_fusion.5
  219.0 1.0 bitcast_dynamic-update-slice_fusion.4
  220.9 2.1 bitcast_dynamic-update-slice_fusion.2
  223.0 2.1 bitcast_dynamic-update-slice_fusion.1
  226.1 11.5 %gather_fusion = bf16[16,1024,384]{2,1,0:T(8,128)(2,1)} fusion(bf16[16,1024,384]{2,1,0:T(8,128)(2,1)} %bitcast_dynamic-update-slice_fusion, s32[1024]{0:T(1024)S(1)} %pad_clamp_fusion), kind=kCustom, calls=%fused_computation | custom fusion | bytes 25165888 | tf_op jit(solution)/shard_map/gather | solution.py:28
  237.6 16.6 %copy.66 = bf16[1024,16,384]{0,2,1:T(8,128)(2,1)} copy(bf16[1024,16,384]{2,0,1:T(8,128)(2,1)} %bitcast.96) | data formatting | bytes 25165824 | tf_op jit(solution)/shard_map/transpose | solution.py:11
  254.2 62.3 %while.10 = (s32[]{:T(128)}, f32[8,128,128]{2,1,0:T(8,128)S(1)}, f32[1]{0:T(128)}, s32[]{:T(128)}, bf16[16,1]{0,1:T(2,128)(2,1)S(1)}, /*index=5*/bf16[16,8]{1,0:...) while((s32[]{:T(128)}, f32[8,128,128]{2,1,0:T(8,128)S(1)}, ...), condition=%wide.region_2.3_spmd.clone, body=%wide.region_1.2_spmd.clone.sunk | while | flops 655388 | bytes 1310999 | solution.py:52
  256.3 1.1 fusion.38
  260.2 1.1 fusion.38
  264.1 1.1 fusion.38
  268.0 1.1 fusion.38
  271.9 1.1 fusion.38
  275.8 1.1 fusion.38
  279.7 1.1 fusion.38
  283.6 1.1 fusion.38
  287.5 1.1 fusion.38
  291.4 1.1 fusion.38
  295.3 1.1 fusion.38
  299.2 1.1 fusion.38
  303.1 1.1 fusion.38
  307.0 1.1 fusion.38
  310.9 1.1 fusion.38
  314.8 1.1 fusion.38
  316.7 1.3 convolution_bitcast_fusion.1
  318.7 10.0 %convolution_convert_fusion = bf16[128,6144]{1,0:T(8,128)(2,1)} fusion(bf16[128,1024]{0,1:T(8,128)(2,1)S(1)} %bitcast.98, bf16[1024,6144]{0,1:T(8,128)(2,1)} %bitcast.95), kind=kOutput, calls=%fused_computation.8 | convolution fusion | flops 1611399168 | bytes 14417920 | tf_op jit(solution)/shard_map/dot_general | solution.py:165
  328.8 75.8 %reduce-scatter.2.cloned.1.call-done = bf16[128,768]{1,0:T(8,128)(2,1)} async-done(((bf16[128,6144]{1,0:T(8,128)(2,1)}), bf16[128,768]{1,0:T(8,128)(2,1)}) %reduce-scatter.2.cloned.1.call-update) | async-done | bytes 196624 | tf_op jit(solution)/shard_map/reduce_scatter | solution.py:168
  404.5 4.7 %collective-permute-start.15 = (bf16[128,768]{1,0:T(8,128)(2,1)}, bf16[128,768]{1,0:T(8,128)(2,1)S(1)}, u32[]{:S(2)}, u32[]{:S(2)}) collective-permute-start(bf16[128,768]{1,0:T(8,128)(2,1)} %reduce-scatter.2.cloned.1.call-done), channel_id=1, source_target_pairs={{0,1},{1,0},{2,3},{3,2},{4,5},{5,4},{6,7},{7,6},{8,9},{9,8},{10,11... | collective-permute-start | bytes 589832 | tf_op jit(solution)/shard_map/ppermute | solution.py:57
  409.2 1.3 collective-permute-done.15
  (101 shorter events, 22.5 us)
Async XLA Ops:
  6.5 208.3 %copy-start = (bf16[1,1024,384]{2,1,0:T(8,128)(2,1)S(1)}, bf16[1,1024,384]{2,1,0:T(8,128)(2,1)}, u32[]{:S(2)}) copy-start(bf16[1,1024,384]{2,1,0:T(8,128)(2,1)} %param.17) | copy-start | bytes 2359300
  6.5 247.7 %all-gather.4.cloned.1.call-start = ((), (), s32[]{:S(2)}) async-start(), calls=%async_computation.2 | async-start | bytes 4456448 | tf_op jit(solution)/shard_map/all_gather | solution.py:35
  6.5 21.4 %collective-permute-start = (bf16[1024,384]{1,0:T(8,128)(2,1)}, bf16[1024,384]{1,0:T(8,128)(2,1)S(1)}, u32[]{:S(2)}, u32[]{:S(2)}) collective-permute-start(bf16[1024,384]{1,0:T(8,128)(2,1)} %bitcast.106), channel_id=1, source_target_pairs={{0,16},{16,32},{32,48},{48,64},{64,80},{80,96},{96,112},{112,128},... | collective-permute-start | bytes 2359304 | tf_op jit(solution)/shard_map/ppermute | solution.py:23
  27.9 0.9 copy-start.1
  28.9 19.2 %collective-permute-start.1 = (bf16[1024,384]{1,0:T(8,128)(2,1)S(1)}, bf16[1024,384]{1,0:T(8,128)(2,1)S(1)}, u32[]{:S(2)}, u32[]{:S(2)}) collective-permute-start(bf16[1024,384]{1,0:T(8,128)(2,1)S(1)} %collective-permute-done), channel_id=1, source_target_pairs={{0,16},{16,32},{32,48},{48,64},{64,80},{80,96},{96,112},{112,128},... | collective-permute-start | bytes 2359304 | tf_op jit(solution)/shard_map/ppermute | solution.py:23
  28.9 25.0 %collective-permute-start.8 = (bf16[1024,384]{1,0:T(8,128)(2,1)}, bf16[1024,384]{1,0:T(8,128)(2,1)S(1)}, u32[]{:S(2)}, u32[]{:S(2)}) collective-permute-start(bf16[1024,384]{1,0:T(8,128)(2,1)} %bitcast.107), channel_id=1, source_target_pairs={{16,0},{32,16},{48,32},{64,48},{80,64},{96,80},{112,96},{128,112},... | collective-permute-start | bytes 2359304 | tf_op jit(solution)/shard_map/ppermute | solution.py:25
  48.1 145.8 %copy-start.4 = (bf16[1024,384]{1,0:T(8,128)(2,1)}, bf16[1024,384]{1,0:T(8,128)(2,1)S(1)}, u32[]{:S(2)}) copy-start(bf16[1024,384]{1,0:T(8,128)(2,1)S(1)} %collective-permute-done.1) | copy-start | bytes 2359300
  48.1 18.4 %collective-permute-start.2 = (bf16[1024,384]{1,0:T(8,128)(2,1)S(1)}, bf16[1024,384]{1,0:T(8,128)(2,1)}, u32[]{:S(2)}, u32[]{:S(2)}) collective-permute-start(bf16[1024,384]{1,0:T(8,128)(2,1)S(1)} %collective-permute-done.1), channel_id=1, source_target_pairs={{0,16},{16,32},{32,48},{48,64},{64,80},{80,96},{96,112},{112,128},... | collective-permute-start | bytes 2359304 | tf_op jit(solution)/shard_map/ppermute | solution.py:23
  53.9 85.6 %copy-start.2 = (bf16[1024,384]{1,0:T(8,128)(2,1)}, bf16[1024,384]{1,0:T(8,128)(2,1)S(1)}, u32[]{:S(2)}) copy-start(bf16[1024,384]{1,0:T(8,128)(2,1)S(1)} %collective-permute-done.8) | copy-start | bytes 2359300
  53.9 17.4 %collective-permute-start.9 = (bf16[1024,384]{1,0:T(8,128)(2,1)S(1)}, bf16[1024,384]{1,0:T(8,128)(2,1)}, u32[]{:S(2)}, u32[]{:S(2)}) collective-permute-start(bf16[1024,384]{1,0:T(8,128)(2,1)S(1)} %collective-permute-done.8), channel_id=1, source_target_pairs={{16,0},{32,16},{48,32},{64,48},{80,64},{96,80},{112,96},{128,112},... | collective-permute-start | bytes 2359304 | tf_op jit(solution)/shard_map/ppermute | solution.py:25
  66.5 17.7 %collective-permute-start.3 = (bf16[1024,384]{1,0:T(8,128)(2,1)}, bf16[1024,384]{1,0:T(8,128)(2,1)}, u32[]{:S(2)}, u32[]{:S(2)}) collective-permute-start(bf16[1024,384]{1,0:T(8,128)(2,1)} %collective-permute-done.2), channel_id=1, source_target_pairs={{0,16},{16,32},{32,48},{48,64},{64,80},{80,96},{96,112},{112,128},... | collective-permute-start | bytes 2359304 | tf_op jit(solution)/shard_map/ppermute | solution.py:23
  67.7 336.9 %reduce-scatter.2.cloned.1.call-start = ((), (), s32[]{:S(2)}) async-start(), calls=%async_computation.1 | async-start | bytes 1769472 | tf_op jit(solution)/shard_map/reduce_scatter | solution.py:168
  71.3 17.5 %collective-permute-start.10 = (bf16[1024,384]{1,0:T(8,128)(2,1)}, bf16[1024,384]{1,0:T(8,128)(2,1)S(1)}, u32[]{:S(2)}, u32[]{:S(2)}) collective-permute-start(bf16[1024,384]{1,0:T(8,128)(2,1)} %collective-permute-done.9), channel_id=1, source_target_pairs={{16,0},{32,16},{48,32},{64,48},{80,64},{96,80},{112,96},{128,112},... | collective-permute-start | bytes 2359304 | tf_op jit(solution)/shard_map/ppermute | solution.py:25
  84.2 19.5 %collective-permute-start.4 = (bf16[1024,384]{1,0:T(8,128)(2,1)}, bf16[1024,384]{1,0:T(8,128)(2,1)S(1)}, u32[]{:S(2)}, u32[]{:S(2)}) collective-permute-start(bf16[1024,384]{1,0:T(8,128)(2,1)} %collective-permute-done.3), channel_id=1, source_target_pairs={{0,16},{16,32},{32,48},{48,64},{64,80},{80,96},{96,112},{112,128},... | collective-permute-start | bytes 2359304 | tf_op jit(solution)/shard_map/ppermute | solution.py:23
  88.8 0.9 copy-start.5
  89.7 20.4 %collective-permute-start.11 = (bf16[1024,384]{1,0:T(8,128)(2,1)S(1)}, bf16[1024,384]{1,0:T(8,128)(2,1)S(1)}, u32[]{:S(2)}, u32[]{:S(2)}) collective-permute-start(bf16[1024,384]{1,0:T(8,128)(2,1)S(1)} %collective-permute-done.10), channel_id=1, source_target_pairs={{16,0},{32,16},{48,32},{64,48},{80,64},{96,80},{112,96},{128,112},... | collective-permute-start | bytes 2359304 | tf_op jit(solution)/shard_map/ppermute | solution.py:25
  103.7 23.8 %copy-start.9 = (bf16[1024,384]{1,0:T(8,128)(2,1)}, bf16[1024,384]{1,0:T(8,128)(2,1)S(1)}, u32[]{:S(2)}) copy-start(bf16[1024,384]{1,0:T(8,128)(2,1)S(1)} %collective-permute-done.4) | copy-start | bytes 2359300
  103.7 16.0 %collective-permute-start.5 = (bf16[1024,384]{1,0:T(8,128)(2,1)S(1)}, bf16[1024,384]{1,0:T(8,128)(2,1)S(1)}, u32[]{:S(2)}, u32[]{:S(2)}) collective-permute-start(bf16[1024,384]{1,0:T(8,128)(2,1)S(1)} %collective-permute-done.4), channel_id=1, source_target_pairs={{0,16},{16,32},{32,48},{48,64},{64,80},{80,96},{96,112},{112,128},... | collective-permute-start | bytes 2359304 | tf_op jit(solution)/shard_map/ppermute | solution.py:23
  110.1 0.9 copy-start.7
  111.0 16.4 %collective-permute-start.12 = (bf16[1024,384]{1,0:T(8,128)(2,1)S(1)}, bf16[1024,384]{1,0:T(8,128)(2,1)}, u32[]{:S(2)}, u32[]{:S(2)}) collective-permute-start(bf16[1024,384]{1,0:T(8,128)(2,1)S(1)} %collective-permute-done.11), channel_id=1, source_target_pairs={{16,0},{32,16},{48,32},{64,48},{80,64},{96,80},{112,96},{128,112},... | collective-permute-start | bytes 2359304 | tf_op jit(solution)/shard_map/ppermute | solution.py:25
  119.7 13.4 %copy-start.10 = (bf16[1024,384]{1,0:T(8,128)(2,1)}, bf16[1024,384]{1,0:T(8,128)(2,1)S(1)}, u32[]{:S(2)}) copy-start(bf16[1024,384]{1,0:T(8,128)(2,1)S(1)} %collective-permute-done.5) | copy-start | bytes 2359300
  119.7 17.1 %collective-permute-start.6 = (bf16[1024,384]{1,0:T(8,128)(2,1)S(1)}, bf16[1024,384]{1,0:T(8,128)(2,1)}, u32[]{:S(2)}, u32[]{:S(2)}) collective-permute-start(bf16[1024,384]{1,0:T(8,128)(2,1)S(1)} %collective-permute-done.5), channel_id=1, source_target_pairs={{0,16},{16,32},{32,48},{48,64},{64,80},{80,96},{96,112},{112,128},... | collective-permute-start | bytes 2359304 | tf_op jit(solution)/shard_map/ppermute | solution.py:23
  127.5 69.0 %collective-permute-start.13 = (bf16[1024,384]{1,0:T(8,128)(2,1)}, bf16[1024,384]{1,0:T(8,128)(2,1)}, u32[]{:S(2)}, u32[]{:S(2)}) collective-permute-start(bf16[1024,384]{1,0:T(8,128)(2,1)} %collective-permute-done.12), channel_id=1, source_target_pairs={{16,0},{32,16},{48,32},{64,48},{80,64},{96,80},{112,96},{128,112},... | collective-permute-start | bytes 2359304 | tf_op jit(solution)/shard_map/ppermute | solution.py:25
  136.8 61.1 %collective-permute-start.7 = (bf16[1024,384]{1,0:T(8,128)(2,1)}, bf16[1024,384]{1,0:T(8,128)(2,1)}, u32[]{:S(2)}, u32[]{:S(2)}) collective-permute-start(bf16[1024,384]{1,0:T(8,128)(2,1)} %collective-permute-done.6), channel_id=1, source_target_pairs={{0,16},{16,32},{32,48},{48,64},{64,80},{80,96},{96,112},{112,128},... | collective-permute-start | bytes 2359304 | tf_op jit(solution)/shard_map/ppermute | solution.py:23
  196.3 19.6 %copy-start.3 = (bf16[1024,384]{1,0:T(8,128)(2,1)S(1)}, bf16[1024,384]{1,0:T(8,128)(2,1)}, u32[]{:S(2)}) copy-start(bf16[1024,384]{1,0:T(8,128)(2,1)} %copy-done.2) | copy-start | bytes 2359300
  196.3 22.7 %copy-start.6 = (bf16[1024,384]{1,0:T(8,128)(2,1)S(1)}, bf16[1024,384]{1,0:T(8,128)(2,1)}, u32[]{:S(2)}) copy-start(bf16[1024,384]{1,0:T(8,128)(2,1)} %copy-done.5) | copy-start | bytes 2359300
  196.3 23.7 %copy-start.8 = (bf16[1024,384]{1,0:T(8,128)(2,1)S(1)}, bf16[1024,384]{1,0:T(8,128)(2,1)}, u32[]{:S(2)}) copy-start(bf16[1024,384]{1,0:T(8,128)(2,1)} %copy-done.7) | copy-start | bytes 2359300
  196.5 28.7 %collective-permute-start.14 = (bf16[1024,384]{1,0:T(8,128)(2,1)}, bf16[1024,384]{1,0:T(8,128)(2,1)S(1)}, u32[]{:S(2)}, u32[]{:S(2)}) collective-permute-start(bf16[1024,384]{1,0:T(8,128)(2,1)} %collective-permute-done.13), channel_id=1, source_target_pairs={{16,0},{32,16},{48,32},{64,48},{80,64},{96,80},{112,96},{128,112},... | collective-permute-start | bytes 2359304 | tf_op jit(solution)/shard_map/ppermute | solution.py:25
  237.6 79.0 %copy-start.12 = (s32[1,128]{1,0:T(1,128)S(1)}, s32[1,128]{1,0:T(1,128)}, u32[]{:S(2)}) copy-start(s32[1,128]{1,0:T(1,128)} %param.15) | copy-start | bytes 1540
  237.6 80.9 %copy-start.11 = (f32[1,1024]{1,0:T(1,128)S(1)}, f32[1,1024]{1,0:T(1,128)}, u32[]{:S(2)}) copy-start(f32[1,1024]{1,0:T(1,128)} %param.16) | copy-start | bytes 12292
  404.5 6.0 %collective-permute-start.15 = (bf16[128,768]{1,0:T(8,128)(2,1)}, bf16[128,768]{1,0:T(8,128)(2,1)S(1)}, u32[]{:S(2)}, u32[]{:S(2)}) collective-permute-start(bf16[128,768]{1,0:T(8,128)(2,1)} %reduce-scatter.2.cloned.1.call-done), channel_id=1, source_target_pairs={{0,1},{1,0},{2,3},{3,2},{4,5},{5,4},{6,7},{7,6},{8,9},{9,8},{10,11... | collective-permute-start | bytes 589832 | tf_op jit(solution)/shard_map/ppermute | solution.py:57
Sparse Core Ops, SparseCore 0:
  67.8 118.9 all-gather.3
  328.9 75.5 reduce-scatter.1
